TPU v7x, 256 devices: a whole 4x4x8 slice. The times are simulated.
256 devices in a mesh: expert: 32 (over y, x, core), tensor: 8 (over z).
Axes of the slice: x: 4, y: 4, z: 8, core: 2. Of those that a mesh axis runs over, the one named last changes fastest.
Arguments:
- tokens: bfloat16 [16384, 4096], P('expert', 'tensor'), may hold values from -36 to 36
- expert_ids: int32 [16384, 1], P('expert'), may hold values from 0 to 63; in each aligned block of 512 rows (0 to 511, 512 to 1023, ...) at most 16 rows name the same one
- gates: float32 [16384, 1], P('expert'), may hold values from 0.25 to 1
- expert_in: bfloat16 [64, 4096, 2048], P('expert', 'tensor'), may hold values from -0.09375 to 0.09375
- expert_out: bfloat16 [64, 2048, 4096], P('expert', None, 'tensor'), may hold values from -0.125 to 0.125
- norm_gain: float32 [4096], replicated, may hold values from 0.5 to 2
- up_weight: bfloat16 [4096, 8192], P('expert', 'tensor'), may hold values from -0.09375 to 0.09375
- down_weight: bfloat16 [4096, 8192], P('expert', 'tensor'), may hold values from -0.0625 to 0.0625
Outputs:
- layer_output: bfloat16 [16384, 4096], P('expert', 'tensor')
Inputs may be any that keep to these rules, and one draw needn't show every extreme that they name: `expert_ids`: among the 512 tokens of one block, at most 16 carry the same expert id; in some blocks one id is carried by exactly 16 tokens.
All inputs are finite; a program needn't handle non-finite values.
Results may differ from a plain program's by a relative error of at most 0.015.
Values may be sent and summed in bfloat16 or wider, within the bound.
No kernel may reach another device: no remote copies, remote signals or barrier semaphores. Data moves between devices by JAX's collectives and lax.ppermute only.
A program may use at most 128 MiB of HBM per device.

v0:
```python
import jax
import jax.numpy as jnp
from jax import lax
from jax.sharding import PartitionSpec as P

EXP_DEV = 2


def slot_table(expert_col, experts, capacity):
    expert = expert_col[:, 0]
    onehot = (expert[:, None] == jnp.arange(experts, dtype=jnp.int32)[None, :]).astype(jnp.int32)
    before = jnp.cumsum(onehot, axis=0) - onehot
    position = jnp.sum(before * onehot, axis=1)
    slot_index = expert * capacity + position
    selector = jnp.arange(experts * capacity, dtype=jnp.int32)[:, None] == slot_index[None, :]
    return selector.astype(jnp.bfloat16)


def trade(buffer):
    result = lax.all_to_all(buffer, "expert", split_axis=0, concat_axis=0, tiled=True)
    return result


def gather_rows(weight, combine, start_value):
    return combine(start_value, lax.all_gather(weight, "expert", axis=0, tiled=True), jnp.int32(0))


def shards(tokens, expert_ids, gates, expert_in, expert_out, norm_gain, up_weight, down_weight):
    token_count = tokens.shape[0]
    local_width = tokens.shape[1]
    groups = lax.axis_size("expert")
    experts = EXP_DEV * groups
    capacity = 2 * token_count // experts
    selector = slot_table(expert_ids, experts, capacity)
    outgoing = jnp.dot(selector, tokens, preferred_element_type=jnp.float32).astype(jnp.bfloat16)
    outgoing = outgoing.reshape(groups, EXP_DEV, capacity, local_width)
    arrived = trade(outgoing)
    partial_value = jnp.einsum(
        "sjcd,jdh->sjch", arrived, expert_in, preferred_element_type=jnp.float32
    )
    summed = lax.psum(partial_value.astype(jnp.bfloat16), "tensor").astype(jnp.float32)
    active = jax.nn.relu(summed).astype(jnp.bfloat16)
    produced = jnp.einsum(
        "sjch,jhd->sjcd", active, expert_out, preferred_element_type=jnp.float32
    ).astype(jnp.bfloat16)
    returned = trade(produced).reshape(experts * capacity, local_width)
    routed = lax.dot_general(
        selector, returned, (((0,), (0,)), ((), ())), preferred_element_type=jnp.float32
    )
    mixed = (tokens.astype(jnp.float32) + gates * routed).astype(jnp.bfloat16)
    whole = lax.all_gather(mixed, "tensor", axis=1, tiled=True)
    whole_f32 = whole.astype(jnp.float32)
    mean_square = jnp.mean(whole_f32 * whole_f32, axis=1, keepdims=True)
    normed = (whole_f32 * lax.rsqrt(mean_square + 1e-06) * norm_gain).astype(jnp.bfloat16)

    def add_up(carry, piece, start):
        return jnp.dot(normed, piece, preferred_element_type=jnp.float32)

    ffn_hidden = gather_rows(
        up_weight, add_up, jnp.zeros((token_count, up_weight.shape[1]), jnp.float32)
    )
    ffn_active = jax.nn.gelu(ffn_hidden, approximate=True).astype(jnp.bfloat16)

    def add_down(carry, piece, start):
        contribution = lax.dot_general(
            ffn_active, piece, (((1,), (1,)), ((), ())), preferred_element_type=jnp.float32
        )
        return contribution

    outputs = gather_rows(
        down_weight, add_down, jnp.zeros((token_count, whole.shape[1]), jnp.float32)
    )
    summed_out = lax.psum_scatter(
        outputs.astype(jnp.bfloat16), "tensor", scatter_dimension=1, tiled=True
    ).astype(jnp.float32)
    return (mixed.astype(jnp.float32) + summed_out).astype(jnp.bfloat16)


def solution(mesh):
    return jax.shard_map(
        shards,
        mesh=mesh,
        in_specs=(
            P("expert", "tensor"),
            P("expert", None),
            P("expert", None),
            P("expert", "tensor", None),
            P("expert", None, "tensor"),
            P(),
            P("expert", "tensor"),
            P("expert", "tensor"),
        ),
        out_specs=P("expert", "tensor"),
        check_vma=False,
    )
```

profile of v0, /device:TPU:1, one launch (start us, length us, event | category | flops | bytes accessed | tf_op | source)
XLA Modules:
  0.0 424.8 jit_solution(10991581283528540992)
XLA Ops:
  6.5 0.7 fusion.42
  7.2 1.2 reduce-window.6
  8.4 0.2 slice_reduce_fusion
  8.7 0.9 fusion.41
  9.7 0.9 multiply_add_fusion
  10.6 1.8 fusion.24
  12.4 25.6 %all_to_all.10 = bf16[32,2,16,512]{3,2,1,0:T(8,128)(2,1)S(1)} all-to-all(bf16[32,2,16,512]{3,2,1,0:T(8,128)(2,1)S(1)} %bitcast.50), channel_id=1, replica_groups=mesh['expert'=32,'tensor'=8] {'expert'}, dimensions={0} | all-to-all | bytes 2097152 | tf_op jit(solution)/shard_map/all_to_all | solution.py:20
  37.9 4.3 %convert_bitcast_fusion = bf16[32,2,16,2048]{3,2,0,1:T(8,128)(2,1)} fusion(bf16[2,512,2048]{2,1,0:T(8,128)(2,1)S(1)} %copy-done.1, bf16[32,2,16,512]{3,2,1,0:T(8,128)(2,1)S(1)} %all_to_all.10), kind=kOutput, calls=%fused_computation.15 | convolution fusion | flops 2149580800 | bytes 9437184 | tf_op jit(solution)/shard_map/sjcd,jdh->sjch/dot_general | solution.py:38
  42.2 0.0 all-reduce.2.cloned.1.call-update
  42.3 0.0 all-gather.4.cloned.1.call-start
  42.3 108.1 %all-reduce.2.cloned.1.call-done = bf16[32,2,16,2048]{3,2,0,1:T(8,128)(2,1)} async-done(((bf16[32,2,16,2048]{3,2,0,1:T(8,128)(2,1)}), bf16[32,2,16,2048]{3,2,0,1:T(8,128)(2,1)}) %all-reduce.2.cloned.1.call-update) | async-done | bytes 4194320 | tf_op jit(solution)/shard_map/psum | solution.py:41
  150.4 5.8 %fusion.30 = bf16[32,2,16,512]{3,2,0,1:T(8,128)(2,1)S(1)} fusion(bf16[2,2048,512]{2,1,0:T(8,128)(2,1)} %param.12, bf16[32,2,16,2048]{3,2,0,1:T(8,128)(2,1)} %all-reduce.2.cloned.1.call-done), kind=kOutput, calls=%fused_computation.30 | convolution fusion | flops 2154299392 | bytes 9437184 | tf_op jit(solution)/shard_map/sjch,jhd->sjcd/dot_general | solution.py:43
  156.2 0.0 copy-start.2
  156.2 0.0 copy-start.4
  156.2 0.1 copy.16
  156.3 24.6 %all_to_all.11 = bf16[32,2,16,512]{3,2,1,0:T(8,128)(2,1)S(1)} all-to-all(bf16[32,2,16,512]{3,2,1,0:T(8,128)(2,1)S(1)} %copy.16), channel_id=1, replica_groups=mesh['expert'=32,'tensor'=8] {'expert'}, dimensions={0} | all-to-all | bytes 2097152 | tf_op jit(solution)/shard_map/all_to_all | solution.py:20
  180.9 1.6 fusion.35
  182.5 0.0 all-gather.4.cloned.1.call-update
  182.5 0.0 all-gather.6.cloned.1.call-start
  182.6 0.7 all-gather.6.cloned.1.call-update
  183.3 0.0 all-gather.8.cloned.1.call-start
  183.3 0.5 all-gather.8.cloned.1.call-update
  183.8 0.2 reduce-scatter.2.cloned.1.call-start
  184.1 48.4 %all-gather.4.cloned.1.call-done = bf16[512,4096]{1,0:T(8,128)(2,1)} async-done(((bf16[512,512]{1,0:T(8,128)(2,1)}), bf16[512,4096]{1,0:T(8,128)(2,1)}) %all-gather.4.cloned.1.call-update) | async-done | bytes 4194320 | tf_op jit(solution)/shard_map/all_gather | solution.py:51
  232.4 3.1 fusion
  235.5 56.4 %all-gather.6.cloned.1.call-done = bf16[4096,1024]{1,0:T(8,128)(2,1)} async-done(((bf16[128,1024]{1,0:T(8,128)(2,1)}), bf16[4096,1024]{1,0:T(8,128)(2,1)}) %all-gather.6.cloned.1.call-update) | async-done | bytes 8388624 | tf_op jit(solution)/shard_map/all_gather | solution.py:25
  292.0 9.6 %fusion.21 = bf16[512,1024]{1,0:T(8,128)(2,1)S(1)} fusion(bf16[4096,1024]{1,0:T(8,128)(2,1)} %all-gather.6.cloned.1.call-done, bf16[512,4096]{1,0:T(8,128)(2,1)} %all-gather.4.cloned.1.call-done, f32[4096]{0:T(1024)S(1)} %copy-done.3, f32[512]{0:T(512)S(1)} %add_rsqrt_fusion), kind=kOutput, calls=%fused_computation.24 | convolution fusion | flops 4308074496 | bytes 13649920 | tf_op jit(solution)/shard_map/dot_general | solution.py:57
  301.6 50.4 %all-gather.8.cloned.1.call-done = bf16[4096,1024]{1,0:T(8,128)(2,1)} async-done(((bf16[128,1024]{1,0:T(8,128)(2,1)}), bf16[4096,1024]{1,0:T(8,128)(2,1)}) %all-gather.8.cloned.1.call-update) | async-done | bytes 8388624 | tf_op jit(solution)/shard_map/all_gather | solution.py:25
  352.0 9.5 %convolution_convert_fusion = bf16[512,4096]{1,0:T(8,128)(2,1)} fusion(bf16[512,1024]{1,0:T(8,128)(2,1)S(1)} %fusion.21, bf16[4096,1024]{1,0:T(8,128)(2,1)} %all-gather.8.cloned.1.call-done), kind=kOutput, calls=%fused_computation.6 | convolution fusion | flops 4297064448 | bytes 13631488 | tf_op jit(solution)/shard_map/dot_general | solution.py:65
  361.5 0.0 reduce-scatter.2.cloned.1.call-update
  361.5 54.7 %reduce-scatter.2.cloned.1.call-done = bf16[512,512]{1,0:T(8,128)(2,1)} async-done(((bf16[512,4096]{1,0:T(8,128)(2,1)}), bf16[512,512]{1,0:T(8,128)(2,1)}) %reduce-scatter.2.cloned.1.call-update) | async-done | bytes 524304 | tf_op jit(solution)/shard_map/reduce_scatter | solution.py:73
  416.3 2.0 add_convert_fusion
  (12 shorter events, 0.1 us)
Async XLA Ops:
  6.5 143.8 %all-reduce.2.cloned.1.call-start = ((), (), s32[]{:S(2)}) async-start(), calls=%async_computation.3 | async-start | bytes 8388608 | tf_op jit(solution)/shard_map/psum | solution.py:41
  8.7 29.2 %copy-start.1 = (bf16[2,512,2048]{2,1,0:T(8,128)(2,1)S(1)}, bf16[2,512,2048]{2,1,0:T(8,128)(2,1)}, u32[]{:S(2)}) copy-start(bf16[2,512,2048]{2,1,0:T(8,128)(2,1)} %param.11) | copy-start | bytes 12582916
  42.3 190.2 %all-gather.4.cloned.1.call-start = ((), (), s32[]{:S(2)}) async-start(), calls=%async_computation.4 | async-start | bytes 4718592 | tf_op jit(solution)/shard_map/all_gather | solution.py:51
  156.2 24.7 %copy-start.2 = (bf16[512,512]{1,0:T(8,128)(2,1)S(1)}, bf16[512,512]{1,0:T(8,128)(2,1)}, u32[]{:S(2)}) copy-start(bf16[512,512]{1,0:T(8,128)(2,1)} %param.8) | copy-start | bytes 1572868
  156.2 24.7 %copy-start.4 = (f32[512,1]{0,1:T(1,128)S(1)}, f32[512,1]{0,1:T(1,128)}, u32[]{:S(2)}) copy-start(f32[512,1]{0,1:T(1,128)} %param.10) | copy-start | bytes 6148
  180.9 111.0 %copy-start.3 = (f32[4096]{0:T(1024)S(1)}, f32[4096]{0:T(1024)}, u32[]{:S(2)}) copy-start(f32[4096]{0:T(1024)} %param.13) | copy-start | bytes 49156
  182.5 109.4 %all-gather.6.cloned.1.call-start = ((), (), s32[]{:S(2)}) async-start(), calls=%async_computation.5 | async-start | bytes 8650752 | tf_op jit(solution)/shard_map/all_gather | solution.py:25
  183.3 168.7 %all-gather.8.cloned.1.call-start = ((), (), s32[]{:S(2)}) async-start(), calls=%async_computation.6 | async-start | bytes 8650752 | tf_op jit(solution)/shard_map/all_gather | solution.py:25
  183.8 232.4 %reduce-scatter.2.cloned.1.call-start = ((), (), s32[]{:S(2)}) async-start(), calls=%async_computation.7 | async-start | bytes 4718592 | tf_op jit(solution)/shard_map/reduce_scatter | solution.py:73
  361.5 54.8 %copy-start = (bf16[512,512]{1,0:T(8,128)(2,1)S(1)}, bf16[512,512]{1,0:T(8,128)(2,1)}, u32[]{:S(2)}) copy-start(bf16[512,512]{1,0:T(8,128)(2,1)} %fusion.35) | copy-start | bytes 1572868
Sparse Core Ops, SparseCore 0:
  42.4 107.9 all-reduce.1
  182.6 49.7 all-gather.3
  235.0 56.9 all-gather.5
  294.4 57.5 all-gather.7
  361.6 54.5 reduce-scatter.1
where the time goes:
time: 425 us
  waiting for transfers between devices  319 us (75%)
  blocking collectives  50.2 us (12%)
  matrix products  32.6 us (8%)
  between operations  13.2 us (3%)
  other arithmetic  8.86 us (2%)
    psum x1, waiting for transfers between devices, shards(): lax.psum(partial_value.astype(jnp.bfloat16), 'tensor').astype(jnp.float32)  108 us
    all_gather x2, waiting for transfers between devices, gather_rows(): lax.all_gather(weight, 'expert', axis=0, tiled=True)  107 us
    reduce_scatter x1, waiting for transfers between devices, shards(): lax.psum_scatter(outputs.astype(jnp.bfloat16), 'tensor', scatter_dimensio...  54.7 us
    all_to_all x2, blocking collectives, trade(): lax.all_to_all(buffer, 'expert', split_axis=0, concat_axis=0, tiled=True)  50.2 us
    all_gather x1, waiting for transfers between devices, shards(): whole = lax.all_gather(mixed, 'tensor', axis=1, tiled=True)  48.4 us
    dot_general x1, matrix products, add_up(): return jnp.dot(normed, piece, preferred_element_type=jnp.float32)  9.58 us
    dot_general x1, matrix products, add_down(): lax.dot_general(ffn_active, piece, (((1,), (1,)), ((), ())), preferred_el...  9.54 us
  transfers between devices with their start and end apart: 5, of which 5 were waited for; matrix products, arithmetic and copies ran while one was open for 3% of the time, Pallas kernels for 0%

commit v1 on v0

--- a/solution.py
+++ b/solution.py
@@ -48,7 +48,14 @@
         selector, returned, (((0,), (0,)), ((), ())), preferred_element_type=jnp.float32
     )
     mixed = (tokens.astype(jnp.float32) + gates * routed).astype(jnp.bfloat16)
-    whole = lax.all_gather(mixed, "tensor", axis=1, tiled=True)
+    ring = [mixed]
+    for hop in range(7):
+        ring.append(lax.ppermute(ring[-1], "tensor", [(dev, (dev + 1) % 8) for dev in range(8)]))
+    whole = jnp.roll(
+        jnp.concatenate(ring[::-1], axis=1),
+        (lax.axis_index("tensor") + 1) * ring[0].shape[1],
+        axis=1,
+    )
     whole_f32 = whole.astype(jnp.float32)
     mean_square = jnp.mean(whole_f32 * whole_f32, axis=1, keepdims=True)
     normed = (whole_f32 * lax.rsqrt(mean_square + 1e-06) * norm_gain).astype(jnp.bfloat16)

time: 425 us -> 368 us (0.87)
  waiting for transfers between devices: 319 us -> 269 us
  blocking collectives: 50.2 us -> 25.6 us
  local copies, waits for them, and re-layouts: 0.33 us -> 10.5 us
  starting transfers between devices: 0.34 us -> 7.78 us
    all_gather x2, waiting for transfers between devices: 107 us -> 0.05 us  [gather_rows(): lax.all_gather(weight, 'expert', axis=0, tiled=True)]
    ppermute x0 -> x7, waiting for transfers between devices: none -> 83.5 us  [shards(): lax.ppermute(ring[-1], 'tensor', [(dev, (dev + 1) % 8) for dev in range(8)])]
    all_gather x1 -> x0, waiting for transfers between devices: 48.4 us -> none  [shards(): whole = lax.all_gather(mixed, 'tensor', axis=1, tiled=True)]
    all_to_all x2 -> x1, blocking collectives: 50.2 us -> 25.6 us  [trade(): lax.all_to_all(buffer, 'expert', split_axis=0, concat_axis=0, tiled=True)]
    all_to_all x0 -> x1, waiting for transfers between devices: none -> 16.9 us  [trade(): lax.all_to_all(buffer, 'expert', split_axis=0, concat_axis=0, tiled=True)]
    unnamed x10 -> x24, local copies, waits for them, and re-layouts: 0.02 us -> 8.15 us
    all_to_all x0 -> x1, starting transfers between devices: none -> 7.55 us  [trade(): lax.all_to_all(buffer, 'expert', split_axis=0, concat_axis=0, tiled=True)]
    reduce_scatter x1, waiting for transfers between devices: 54.7 us -> 60.2 us  [shards(): lax.psum_scatter(outputs.astype(jnp.bfloat16), 'tensor', scatter_dimensio...]
  transfers between devices with their start and end apart: 5 -> 12, of which waited for: 5 -> 10; matrix products, arithmetic and copies ran while one was open for 3% -> 6% of each run, Pallas kernels for 0% -> 0%
where the time goes in v1:
time: 368 us
  waiting for transfers between devices  269 us (73%)
  matrix products  34.4 us (9%)
  blocking collectives  25.6 us (7%)
  between operations  15.1 us (4%)
  local copies, waits for them, and re-layouts  10.5 us (3%)
  starting transfers between devices  7.78 us (2%)
  other arithmetic  5.55 us (2%)
    psum x1, waiting for transfers between devices, shards(): lax.psum(partial_value.astype(jnp.bfloat16), 'tensor').astype(jnp.float32)  107 us
    ppermute x7, waiting for transfers between devices, shards(): lax.ppermute(ring[-1], 'tensor', [(dev, (dev + 1) % 8) for dev in range(8)])  83.5 us
    reduce_scatter x1, waiting for transfers between devices, shards(): lax.psum_scatter(outputs.astype(jnp.bfloat16), 'tensor', scatter_dimensio...  60.2 us
    all_to_all x1, blocking collectives, trade(): lax.all_to_all(buffer, 'expert', split_axis=0, concat_axis=0, tiled=True)  25.6 us
    all_to_all x1, waiting for transfers between devices, trade(): lax.all_to_all(buffer, 'expert', split_axis=0, concat_axis=0, tiled=True)  16.9 us
    dot_general x1, matrix products, add_up(): return jnp.dot(normed, piece, preferred_element_type=jnp.float32)  9.65 us
    dot_general x1, matrix products, add_down(): lax.dot_general(ffn_active, piece, (((1,), (1,)), ((), ())), preferred_el...  9.54 us
    unnamed x24, local copies, waits for them, and re-layouts  8.15 us
  transfers between devices with their start and end apart: 12, of which 10 were waited for; matrix products, arithmetic and copies ran while one was open for 6% of the time, Pallas kernels for 0%

profile of v1, /device:TPU:1, one launch (start us, length us, event | category | flops | bytes accessed | tf_op | source)
XLA Modules:
  0.0 367.6 jit_solution(741552275235842413)
XLA Ops:
  7.4 0.7 fusion.43
  8.1 1.2 reduce-window.6
  9.5 0.8 fusion.42
  10.3 0.7 multiply_add_fusion
  11.0 1.8 fusion.27
  12.8 25.6 %all_to_all.10 = bf16[32,2,16,512]{3,2,1,0:T(8,128)(2,1)S(1)} all-to-all(bf16[32,2,16,512]{3,2,1,0:T(8,128)(2,1)S(1)} %bitcast.50), channel_id=1, replica_groups=mesh['expert'=32,'tensor'=8] {'expert'}, dimensions={0} | all-to-all | bytes 2097152 | tf_op jit(solution)/shard_map/all_to_all | solution.py:20
  38.4 6.6 %convert_bitcast_fusion = bf16[32,2,16,2048]{3,2,0,1:T(8,128)(2,1)} fusion(bf16[2,512,2048]{2,1,0:T(8,128)(2,1)} %param.11, bf16[32,2,16,512]{3,2,1,0:T(8,128)(2,1)S(1)} %all_to_all.10), kind=kOutput, calls=%fused_computation.15 | convolution fusion | flops 2149580800 | bytes 9437184 | tf_op jit(solution)/shard_map/sjcd,jdh->sjch/dot_general | solution.py:38
  45.6 0.5 all-gather.5.cloned.1.call-update
  46.1 106.9 %all-reduce.2.cloned.1.call-done = bf16[32,2,16,2048]{3,2,0,1:T(8,128)(2,1)} async-done(((bf16[32,2,16,2048]{3,2,0,1:T(8,128)(2,1)}), bf16[32,2,16,2048]{3,2,0,1:T(8,128)(2,1)}) %all-reduce.2.cloned.1.call-update) | async-done | bytes 4194320 | tf_op jit(solution)/shard_map/psum | solution.py:41
  153.1 6.1 %fusion.31 = bf16[32,2,16,512]{3,2,0,1:T(8,128)(2,1)S(1)} fusion(bf16[2,2048,512]{2,1,0:T(8,128)(2,1)} %param.12, bf16[32,2,16,2048]{3,2,0,1:T(8,128)(2,1)} %all-reduce.2.cloned.1.call-done), kind=kOutput, calls=%fused_computation.31 | convolution fusion | flops 2154299392 | bytes 9437184 | tf_op jit(solution)/shard_map/sjch,jhd->sjcd/dot_general | solution.py:43
  159.2 1.0 copy.26
  160.2 7.6 %all-to-all-start.1 = ((bf16[32,2,16,512]{3,2,1,0:T(8,128)(2,1)}), bf16[32,2,16,512]{3,2,1,0:T(8,128)(2,1)S(1)}, u32[]{:S(2)}, u32[]{:S(2)}) async-start(bf16[32,2,16,512]{3,2,1,0:T(8,128)(2,1)} %copy.26), calls=%async_computation.1 | async-start | bytes 2097152 | tf_op jit(solution)/shard_map/all_to_all | solution.py:20
  168.1 16.9 %all-to-all-done.1 = bf16[32,2,16,512]{3,2,1,0:T(8,128)(2,1)S(1)} async-done(((bf16[32,2,16,512]{3,2,1,0:T(8,128)(2,1)}), bf16[32,2,16,512]{3,2,1,0:T(8,128)(2,1)S(1)}, u32[]{:S(2)}, u32[]{:S(2)}) %all-to-all-start.1) | async-done | bytes 1048608 | tf_op jit(solution)/shard_map/all_to_all | solution.py:20
  185.0 0.8 fusion.36
  185.8 14.3 %collective-permute-done = bf16[512,512]{0,1:T(8,128)(2,1)S(1)} collective-permute-done((bf16[512,512]{0,1:T(8,128)(2,1)S(1)}, bf16[512,512]{0,1:T(8,128)(2,1)S(1)}, u32[]{:S(2)}, u32[]{:S(2)}) %collective-permute-start) | collective-permute-done | bytes 524320 | tf_op jit(solution)/shard_map/ppermute | solution.py:53
  200.2 13.4 %collective-permute-done.1 = bf16[512,512]{0,1:T(8,128)(2,1)S(1)} collective-permute-done((bf16[512,512]{0,1:T(8,128)(2,1)S(1)}, bf16[512,512]{0,1:T(8,128)(2,1)S(1)}, u32[]{:S(2)}, u32[]{:S(2)}) %collective-permute-start.1) | collective-permute-done | bytes 524320 | tf_op jit(solution)/shard_map/ppermute | solution.py:53
  213.6 12.5 %collective-permute-done.2 = bf16[512,512]{0,1:T(8,128)(2,1)S(1)} collective-permute-done((bf16[512,512]{0,1:T(8,128)(2,1)S(1)}, bf16[512,512]{0,1:T(8,128)(2,1)S(1)}, u32[]{:S(2)}, u32[]{:S(2)}) %collective-permute-start.2) | collective-permute-done | bytes 524320 | tf_op jit(solution)/shard_map/ppermute | solution.py:53
  226.0 11.6 %collective-permute-done.3 = bf16[512,512]{0,1:T(8,128)(2,1)S(1)} collective-permute-done((bf16[512,512]{0,1:T(8,128)(2,1)S(1)}, bf16[512,512]{0,1:T(8,128)(2,1)S(1)}, u32[]{:S(2)}, u32[]{:S(2)}) %collective-permute-start.3) | collective-permute-done | bytes 524320 | tf_op jit(solution)/shard_map/ppermute | solution.py:53
  237.6 10.6 %collective-permute-done.4 = bf16[512,512]{0,1:T(8,128)(2,1)S(1)} collective-permute-done((bf16[512,512]{0,1:T(8,128)(2,1)S(1)}, bf16[512,512]{0,1:T(8,128)(2,1)S(1)}, u32[]{:S(2)}, u32[]{:S(2)}) %collective-permute-start.4) | collective-permute-done | bytes 524320 | tf_op jit(solution)/shard_map/ppermute | solution.py:53
  248.2 10.5 %collective-permute-done.5 = bf16[512,512]{0,1:T(8,128)(2,1)} collective-permute-done((bf16[512,512]{0,1:T(8,128)(2,1)S(1)}, bf16[512,512]{0,1:T(8,128)(2,1)}, u32[]{:S(2)}, u32[]{:S(2)}) %collective-permute-start.5) | collective-permute-done | bytes 524320 | tf_op jit(solution)/shard_map/ppermute | solution.py:53
  258.7 10.7 %collective-permute-done.6 = bf16[512,512]{0,1:T(8,128)(2,1)} collective-permute-done((bf16[512,512]{0,1:T(8,128)(2,1)}, bf16[512,512]{0,1:T(8,128)(2,1)}, u32[]{:S(2)}, u32[]{:S(2)}) %collective-permute-start.6) | collective-permute-done | bytes 524320 | tf_op jit(solution)/shard_map/ppermute | solution.py:53
  269.4 1.1 constant_dynamic-update-slice_fusion.15
  270.5 1.1 constant_dynamic-update-slice_fusion.14
  271.8 1.1 constant_dynamic-update-slice_fusion.7
  272.9 1.1 constant_dynamic-update-slice_fusion.6
  274.3 3.2 copy-done
  277.5 0.9 fusion
  278.5 9.6 %fusion.22 = bf16[512,1024]{1,0:T(8,128)(2,1)S(1)} fusion(bf16[4096,1024]{1,0:T(8,128)(2,1)} %all-gather.3.cloned.1.call-done, f32[4096]{0:T(1024)S(1)} %copy-done.2, f32[512]{0:T(512)S(1)} %add_rsqrt_fusion, bf16[512,8192]{0,1:T(8,128)(2,1)} %copy-done, s32[]{:T(128)S(6)} %select_n.14), kind=kOutput, calls=%fused_computation.25 | convolution fusion | flops 4308074496 | bytes 13649924 | tf_op jit(solution)/shard_map/dot_general | solution.py:64
  288.2 9.5 %convolution_convert_fusion = bf16[512,4096]{0,1:T(8,128)(2,1)} fusion(bf16[512,1024]{1,0:T(8,128)(2,1)S(1)} %fusion.22, bf16[4096,1024]{1,0:T(8,128)(2,1)} %all-gather.5.cloned.1.call-done), kind=kOutput, calls=%fused_computation.6 | convolution fusion | flops 4297064448 | bytes 13631488 | tf_op jit(solution)/shard_map/dot_general | solution.py:72
  297.7 60.2 %reduce-scatter.2.cloned.1.call-done = bf16[512,512]{0,1:T(8,128)(2,1)} async-done(((bf16[512,4096]{0,1:T(8,128)(2,1)}), bf16[512,512]{0,1:T(8,128)(2,1)}) %reduce-scatter.2.cloned.1.call-update) | async-done | bytes 524304 | tf_op jit(solution)/shard_map/reduce_scatter | solution.py:80
  358.0 1.2 add_convert_fusion
  359.2 1.0 copy.28
  (40 shorter events, 1.8 us)
Async XLA Ops:
  7.4 145.7 %all-reduce.2.cloned.1.call-start = ((), (), s32[]{:S(2)}) async-start(), calls=%async_computation.3 | async-start | bytes 8388608 | tf_op jit(solution)/shard_map/psum | solution.py:41
  44.9 233.5 %all-gather.3.cloned.1.call-start = ((), (), s32[]{:S(2)}) async-start(), calls=%async_computation.4 | async-start | bytes 8650752 | tf_op jit(solution)/shard_map/all_gather | solution.py:25
  45.5 242.6 %all-gather.5.cloned.1.call-start = ((), (), s32[]{:S(2)}) async-start(), calls=%async_computation.5 | async-start | bytes 8650752 | tf_op jit(solution)/shard_map/all_gather | solution.py:25
  46.1 121.7 %copy-start.1 = (bf16[512,512]{1,0:T(8,128)(2,1)S(1)}, bf16[512,512]{1,0:T(8,128)(2,1)}, u32[]{:S(2)}) copy-start(bf16[512,512]{1,0:T(8,128)(2,1)} %param.8) | copy-start | bytes 1572868
  46.1 138.8 %copy-start.3 = (f32[512,1]{0,1:T(1,128)S(1)}, f32[512,1]{0,1:T(1,128)}, u32[]{:S(2)}) copy-start(f32[512,1]{0,1:T(1,128)} %param.10) | copy-start | bytes 6148
  160.2 24.7 %all-to-all-start.1 = ((bf16[32,2,16,512]{3,2,1,0:T(8,128)(2,1)}), bf16[32,2,16,512]{3,2,1,0:T(8,128)(2,1)S(1)}, u32[]{:S(2)}, u32[]{:S(2)}) async-start(bf16[32,2,16,512]{3,2,1,0:T(8,128)(2,1)} %copy.26), calls=%async_computation.1 | async-start | bytes 2097152 | tf_op jit(solution)/shard_map/all_to_all | solution.py:20
  167.8 190.2 %reduce-scatter.2.cloned.1.call-start = ((), (), s32[]{:S(2)}) async-start(), calls=%async_computation.6 | async-start | bytes 4718592 | tf_op jit(solution)/shard_map/reduce_scatter | solution.py:80
  185.8 14.4 %collective-permute-start = (bf16[512,512]{0,1:T(8,128)(2,1)S(1)}, bf16[512,512]{0,1:T(8,128)(2,1)S(1)}, u32[]{:S(2)}, u32[]{:S(2)}) collective-permute-start(bf16[512,512]{0,1:T(8,128)(2,1)S(1)} %fusion.36), channel_id=1, source_target_pairs={{0,1},{1,2},{2,3},{3,4},{4,5},{5,6},{6,7},{7,0},{8,9},{9,10},{10,1... | collective-permute-start | bytes 1572872 | tf_op jit(solution)/shard_map/ppermute | solution.py:53
  200.2 13.4 %collective-permute-start.1 = (bf16[512,512]{0,1:T(8,128)(2,1)S(1)}, bf16[512,512]{0,1:T(8,128)(2,1)S(1)}, u32[]{:S(2)}, u32[]{:S(2)}) collective-permute-start(bf16[512,512]{0,1:T(8,128)(2,1)S(1)} %collective-permute-done), channel_id=1, source_target_pairs={{0,1},{1,2},{2,3},{3,4},{4,5},{5,6},{6,7},{7,0},{8,9},{9,10},{10,1... | collective-permute-start | bytes 1572872 | tf_op jit(solution)/shard_map/ppermute | solution.py:53
  213.6 12.5 %collective-permute-start.2 = (bf16[512,512]{0,1:T(8,128)(2,1)S(1)}, bf16[512,512]{0,1:T(8,128)(2,1)S(1)}, u32[]{:S(2)}, u32[]{:S(2)}) collective-permute-start(bf16[512,512]{0,1:T(8,128)(2,1)S(1)} %collective-permute-done.1), channel_id=1, source_target_pairs={{0,1},{1,2},{2,3},{3,4},{4,5},{5,6},{6,7},{7,0},{8,9},{9,10},{10,1... | collective-permute-start | bytes 1572872 | tf_op jit(solution)/shard_map/ppermute | solution.py:53
  226.0 11.6 %collective-permute-start.3 = (bf16[512,512]{0,1:T(8,128)(2,1)S(1)}, bf16[512,512]{0,1:T(8,128)(2,1)S(1)}, u32[]{:S(2)}, u32[]{:S(2)}) collective-permute-start(bf16[512,512]{0,1:T(8,128)(2,1)S(1)} %collective-permute-done.2), channel_id=1, source_target_pairs={{0,1},{1,2},{2,3},{3,4},{4,5},{5,6},{6,7},{7,0},{8,9},{9,10},{10,1... | collective-permute-start | bytes 1572872 | tf_op jit(solution)/shard_map/ppermute | solution.py:53
  237.6 10.6 %collective-permute-start.4 = (bf16[512,512]{0,1:T(8,128)(2,1)S(1)}, bf16[512,512]{0,1:T(8,128)(2,1)S(1)}, u32[]{:S(2)}, u32[]{:S(2)}) collective-permute-start(bf16[512,512]{0,1:T(8,128)(2,1)S(1)} %collective-permute-done.3), channel_id=1, source_target_pairs={{0,1},{1,2},{2,3},{3,4},{4,5},{5,6},{6,7},{7,0},{8,9},{9,10},{10,1... | collective-permute-start | bytes 1572872 | tf_op jit(solution)/shard_map/ppermute | solution.py:53
  248.2 10.5 %collective-permute-start.5 = (bf16[512,512]{0,1:T(8,128)(2,1)S(1)}, bf16[512,512]{0,1:T(8,128)(2,1)}, u32[]{:S(2)}, u32[]{:S(2)}) collective-permute-start(bf16[512,512]{0,1:T(8,128)(2,1)S(1)} %collective-permute-done.4), channel_id=1, source_target_pairs={{0,1},{1,2},{2,3},{3,4},{4,5},{5,6},{6,7},{7,0},{8,9},{9,10},{10,1... | collective-permute-start | bytes 1572872 | tf_op jit(solution)/shard_map/ppermute | solution.py:53
  258.7 10.7 %collective-permute-start.6 = (bf16[512,512]{0,1:T(8,128)(2,1)}, bf16[512,512]{0,1:T(8,128)(2,1)}, u32[]{:S(2)}, u32[]{:S(2)}) collective-permute-start(bf16[512,512]{0,1:T(8,128)(2,1)} %collective-permute-done.5), channel_id=1, source_target_pairs={{0,1},{1,2},{2,3},{3,4},{4,5},{5,6},{6,7},{7,0},{8,9},{9,10},{10,1... | collective-permute-start | bytes 1572872 | tf_op jit(solution)/shard_map/ppermute | solution.py:53
  271.7 6.8 %copy-start.2 = (f32[4096]{0:T(1024)S(1)}, f32[4096]{0:T(1024)}, u32[]{:S(2)}) copy-start(f32[4096]{0:T(1024)} %param.13) | copy-start | bytes 49156
  274.3 3.2 copy-start
Sparse Core Ops, SparseCore 0:
  45.1 107.9 all-reduce.1
  297.8 60.0 reduce-scatter.1
Sparse Core Ops, SparseCore 1:
  48.0 57.1 all-gather.2
  107.6 57.4 all-gather.4
